TPU v7x, 128 devices: a whole 4x4x4 slice. The times are simulated.
128 devices in a mesh: row: 16 (over x, z_lo, core), col: 8 (over z_hi, y).
Axes of the slice: x: 4, y: 4, z: 4 (z_hi: 2, z_lo: 2; z = z_hi * 2 + z_lo), core: 2. Of those that a mesh axis runs over, the one named last changes fastest.
Arguments:
- amplitudes: bfloat16 [3, 1024, 16384], P(None, 'row', 'col'), may hold values from -6 to 6
- integrals: bfloat16 [5, 16384, 16384], P(None, 'col', 'row'), may hold values from -0.046875 to 0.046875
- tile_pairs: int32 [5, 2], replicated, may hold values from 0 to 2, as said below
- driving: bfloat16 [3, 1024, 16384], P(None, 'col', 'row'), may hold values from -6 to 6
- occupied_energy: float32 [32], replicated, may hold values from -1 to -0.2
- virtual_energy: float32 [3, 2, 128], replicated, may hold values from 0.3 to 2
Outputs:
- residual: float32 [3, 1024, 16384], P(None, 'col', 'row')
- update: float32 [3, 1024, 16384], P(None, 'col', 'row')
Inputs may be any that keep to these rules, and one draw needn't show every extreme that they name: `tile_pairs`: the 3 tiles fall into two symmetry sectors, two tiles in one and one in the other; each ordered pair of tiles within a sector is one row, in an order drawn from the seed.
All inputs are finite; a program needn't handle non-finite values.
Results may differ from a plain program's by a relative error of at most 0.0003.
Values may be sent and summed in bfloat16 or wider, within the bound.
A program may use at most 192 MiB of HBM per device.

v0:
```python
import functools

import jax
import jax.numpy as jnp
from jax import lax
from jax.experimental import pallas as pl
from jax.experimental.pallas import tpu as pltpu
from jax.sharding import PartitionSpec as P

MESH = pl.DeviceIdType.MESH
NB = 8
QN = 256
RN = 4
ROUNDS = 12
SET = 144
HALF = 80
WIDE = QN + QN // 2
LEVELS = 10
LONE_LAGS, LAGS, Z_LAGS = (2, 7, 10, 14), (1, 3, 6, 9), (3, 4, 7, 9)
ZROUNDS = 1
GAP = 4


def encode(ref, value):
    lead = value.astype(jnp.bfloat16)
    wide = lead.astype(jnp.float32)
    safe = jnp.where(jnp.abs(wide) < 1e-36, 1.0, wide)
    steps = jnp.round((value - wide) * pl.reciprocal(safe, approx=True) * (256.0 * LEVELS))
    steps = jnp.clip(steps, -LEVELS, LEVELS)
    half = QN // 2
    ref[:, :QN] = lead
    ref[:, QN:] = (steps[:, :half] * (2 * LEVELS + 1) + steps[:, half:]).astype(jnp.bfloat16)


def decode(ref):
    wide = ref[:, :QN].astype(jnp.float32)
    code = ref[:, QN:].astype(jnp.float32)
    first = jnp.round(code * (1.0 / (2 * LEVELS + 1)))
    second = code - first * (2 * LEVELS + 1)
    return wide + wide * (jnp.concatenate([first, second], axis=1) * (1.0 / (256.0 * LEVELS)))


def read_pairs(tp_ref):
    pairs = tp_ref[...]
    src = [pairs[0, e] for e in range(5)]
    dst = [pairs[1, e] for e in range(5)]
    counts = [sum((src[e] == v).astype(jnp.int32) for e in range(5)) for v in range(3)]
    return src, dst, jnp.where(counts[0] == 1, 0, jnp.where(counts[1] == 1, 1, 2))


def kernel(
    tp_ref, amp_hbm, int_hbm, out_hbm,
    g, wt, s_buf, t, t_far, fwd_out, fwd, rcv_out, rcv, zf_out, zf, zr_out, zr, f, xr_out, xr, lad_ref, amp_ref,
    int_sem, z_sem, x_sem, f_sem, t_sem, fwd_sem, rcv_sem, zr_sem, xr_sem, send_sem, own_sem,
):
    row, col = lax.axis_index("row"), lax.axis_index("col")
    x, zl, k = row // 4, (row // 2) % 2, row % 2
    zh, y = col // 4, col % 4

    def at_row(xx, zz, kk):
        return (xx * 4 + zz * 2 + kk, col)

    def at_col(cc):
        return (row, cc)

    xp, xm, xo = (x + 1) % 4, (x + 3) % 4, (x + 2) % 4
    yp, ym, yo = (y + 1) % 4, (y + 3) % 4, (y + 2) % 4
    right, left = at_row(xp, zl, k), at_row(xm, zl, k)
    zpart, twin = at_row(x, 1 - zl, k), at_row(x, zl, 1 - k)
    up, down = at_col(zh * 4 + yp), at_col(zh * 4 + ym)
    far = at_col((1 - zh) * 4 + y)

    load_own = pltpu.make_async_copy(amp_hbm, amp_ref, own_sem.at[3])
    load_own.start()

    barrier = pltpu.get_barrier_semaphore()
    partners = [right, left, zpart, twin] + [at_col((col + d) % NB) for d in range(1, NB)]
    for p in partners:
        pl.semaphore_signal(barrier, inc=1, device_id=p, device_id_type=MESH)
    load = pltpu.make_async_copy(int_hbm, wt, int_sem)
    load.start()

    src, dst, lone = read_pairs(tp_ref)
    first = jnp.where(lone == 0, 1, 0)
    second = jnp.where(lone == 2, 1, 2)

    def entry(a, b):
        found = jnp.int32(0)
        for e in range(1, 5):
            found = jnp.where((src[e] == a) & (dst[e] == b), e, found)
        return found

    e_l = entry(lone, lone)
    e_ff, e_sf = entry(first, first), entry(second, first)
    e_fs, e_ss = entry(first, second), entry(second, second)

    own = x * 2 + zl
    to = lax.broadcasted_iota(jnp.int32, (64, 64), 0)
    frm = lax.broadcasted_iota(jnp.int32, (64, 64), 1)
    block, mid, low = to // 8, (to // 2) % 2, to % 2
    distance = (block + NB - own) % NB
    direct = (distance < 4) | ((distance == 4) & (block >= 4))
    ilo, jlo = jnp.where(direct, mid, low), jnp.where(direct, low, mid)
    order64 = (frm == ilo * 32 + block * 4 + ((to // 4) % 2) * 2 + jlo).astype(jnp.bfloat16)
    load_own.wait()
    for s, tile in ((0, lone), (2, second), (1, first)):
        g[s, own, k] = jnp.dot(order64, amp_ref[tile], preferred_element_type=jnp.float32).astype(jnp.bfloat16)
    pl.semaphore_wait(barrier, len(partners))

    def rdma(ref_src, ref_dst, ss, rs, dev):
        return pltpu.make_async_remote_copy(
            src_ref=ref_src, dst_ref=ref_dst, send_sem=ss, recv_sem=rs, device_id=dev, device_id_type=MESH
        )

    def chip(xx, zz):
        return xx * 2 + zz

    def cz(s, a, i=0):
        return rdma(g.at[s, a, k], g.at[s, a, k], send_sem.at[0], z_sem.at[s + i], zpart)

    def cx(s, a, side, which):
        return rdma(g.at[s, a, k], g.at[s, a, k], send_sem.at[1], x_sem.at[s, side, which], right if side == 0 else left)

    def cf(s, a, side, which):
        part = g.at[s, a, k, pl.ds(32 * side, 32)]
        return rdma(part, part, send_sem.at[2], f_sem.at[s, which], right if side == 0 else left)

    def far_arrived(s, which):
        whole = g.at[s, fars[which], k]
        rdma(whole, whole, send_sem.at[2], f_sem.at[s, which], right).wait_recv()

    def ct(s, a):
        return rdma(g.at[s, a, k], g.at[s, a, k], send_sem.at[3], t_sem.at[s], twin)

    own_z = chip(x, 1 - zl)
    lefts, rights = (chip(xm, zl), chip(xm, 1 - zl)), (chip(xp, zl), chip(xp, 1 - zl))
    fars = (chip(xo, zl), chip(xo, 1 - zl))

    def send_own_z(s):
        cz(s, own).start()

    def send_own_x(s):
        cx(s, own, 0, 0).start()
        cx(s, own, 1, 0).start()
        ct(s, own).start()

    def pass_z(s):
        cz(s, own_z).wait_recv()
        cx(s, own_z, 0, 1).start()
        cx(s, own_z, 1, 1).start()
        ct(s, own_z).start()

    def pass_x(s, which):
        cx(s, lefts[which], 0, which).wait_recv()
        cf(s, lefts[which], 0, which).start()
        ct(s, lefts[which]).start()
        cx(s, rights[which], 1, which).wait_recv()
        cf(s, rights[which], 1, which).start()
        ct(s, rights[which]).start()

    def pass_far(s):
        for which in range(2):
            far_arrived(s, which)
            ct(s, fars[which]).start()

    def end_twin(s):
        half = g.at[s, :, 1 - k]
        rdma(half, half, send_sem.at[3], t_sem.at[s], twin).wait_recv()

    def straight(s):
        cx(s, own, 0, 0).start()
        cx(s, own, 1, 0).start()
        ct(s, own).start()

    def straight_pass(s):
        cx(s, lefts[0], 0, 0).wait_recv()
        cf(s, lefts[0], 0, 0).start()
        cx(s, rights[0], 1, 0).wait_recv()
        cf(s, rights[0], 1, 0).start()
        cz(s, lefts[0], 1).start()
        cz(s, rights[0], 2).start()
        ct(s, lefts[0]).start()
        ct(s, rights[0]).start()

    def straight_far(s):
        far_arrived(s, 0)
        cz(s, fars[0], 3).start()
        ct(s, fars[0]).start()

    def straight_across(s, i, a):
        cz(s, a, i).wait_recv()
        ct(s, a).start()

    def sent(ref, i):
        rdma(ref, ref, send_sem.at[i], z_sem.at[0], twin).wait_send()

    def end_sends():
        sent(g.at[0, 0:7, 0], 0)
        sent(g.at[0, 0:5], 1)
        sent(g.at[0, 0:2], 2)
        sent(g.at[:, :, 0], 3)
        sent(fwd_out.at[0 : ROUNDS - ZROUNDS], 4)
        sent(fwd_out.at[0:ZROUNDS, pl.ds(0, HALF)], 5)
        sent(rcv_out.at[0 : ROUNDS - ZROUNDS], 6)
        sent(rcv_out.at[0:ZROUNDS, :, pl.ds(0, HALF)], 7)
        sent(zr.at[0 : ROUNDS - ZROUNDS], 8)
        sent(zf_out, 9)

        @pl.when(zh == 0)
        def _():
            sent(xr_out, 10)

        @pl.when(zh == 1)
        def _():
            sent(xr_out.at[:, 0:3], 10)

    def c_fwd(r, side, zfirst, odd=0):
        if zfirst:
            rows = pl.ds(48 * side, 48 - 16 * side)
        else:
            rows = pl.ds(0, HALF) if side != odd else pl.ds(HALF, SET - HALF)
        return rdma(
            fwd_out.at[r, rows], fwd.at[r, rows], send_sem.at[4 + zfirst], fwd_sem.at[r], up if side == 0 else down
        )

    def c_rcv(r, side, zfirst):
        rows = pl.ds(0, HALF if zfirst else SET)
        return rdma(
            rcv_out.at[r, side, rows], rcv.at[r, side, rows],
            send_sem.at[6 + zfirst], rcv_sem.at[r], up if side == 0 else down,
        )

    def arrived(ref, sem):
        rdma(ref, ref, send_sem.at[4], sem, twin).wait_recv()

    def c_zr(r):
        return rdma(zr_out.at[r], zr.at[r], send_sem.at[8], zr_sem.at[r], far)

    def c_zf(q, r):
        return rdma(zf_out.at[q], zf.at[q], send_sem.at[9], zr_sem.at[r], far)

    def c_xr(r, d):
        return rdma(xr_out.at[r, d - 1], xr.at[r, d - 1], send_sem.at[10], xr_sem.at[r], at_col((col + d) % NB))

    def zfirst_of(r):
        return (r > RN) & (r < RN + 2 * ZROUNDS) & (r % 2 == 1)

    def both(stage, zstage):
        def run(r):
            pl.when(jnp.logical_not(zfirst_of(r)))(lambda: stage(r))
            pl.when(zfirst_of(r))(lambda: zstage(r, (r - RN) // 2))

        return run

    def mine(at):
        return pl.ds(pl.multiple_of(64 * zh + at, 16), 16)

    def others(at):
        return pl.ds(pl.multiple_of(64 * (1 - zh) + at, 16), 16)

    def make_block(c, d):
        b = (c + d) % NB
        direct = s_buf[c, :, b]
        if d == 0:
            return direct
        other = s_buf[b, :, c]
        mirrored = jnp.stack(
            [
                jnp.concatenate([other[0, :4], other[1, :4]], axis=0),
                jnp.concatenate([other[0, 4:], other[1, 4:]], axis=0),
            ]
        )
        return direct + mirrored

    def stage1(r, pairs):
        n = r % RN
        columns = pl.ds(pl.multiple_of(n * QN, QN), QN)
        for m in range(4):
            total = None
            for slot, e in pairs:
                lhs = g[slot, 2 * m : 2 * m + 2].reshape(256, 2048)
                part = jnp.dot(lhs, wt[e, :, columns], preferred_element_type=jnp.float32)
                total = part if total is None else total + part
            s_buf[2 * m : 2 * m + 2] = total.reshape(2, 2, 8, 8, QN)
        def form(store, after_far=lambda: None):
            for rel, yy in enumerate((yo, yp, ym, y)):
                at = 0
                for zz in range(2):
                    for d in range(5 - zz):
                        store(rel, pl.ds(at, 16), make_block(zz * 4 + yy, d).reshape(16, QN))
                        at += 16
                if rel == 0:
                    after_far()

        def form_y(r):
            def store(rel, rows, value):
                if rel == 0:
                    encode(fwd_out.at[r, rows], value)
                else:
                    t[r, rel - 1, rows] = value

            def send():
                for odd in range(2):
                    @pl.when(r % 2 == odd)
                    def _(odd=odd):
                        c_fwd(r, 0, 0, odd).start()
                        c_fwd(r, 1, 0, odd).start()

            form(store, send)

        def form_z(r, q):
            def store(rel, rows, value):
                if rel == 0:
                    t_far[q, rows] = value
                else:
                    t[r, rel - 1, rows] = value

            form(store)
            for at in range(0, HALF, 16):
                encode(zf_out.at[q, 0, pl.ds(at, 16)], t_far[q, others(at)])
                for rel in range(3):
                    encode(zf_out.at[q, 1 + rel, pl.ds(at, 16)], t[r, rel, others(at)])
            c_zf(q, r).start()

        if len(pairs) == 1:
            form_y(r)
        else:
            both(form_y, form_z)(r)

    def stage2_y(r):
        arrived(fwd.at[r], fwd_sem.at[r])

        def pass_on(odd):
            for side in range(2):
                for at in range(0, SET, 16):
                    rows = pl.ds(at, 16)
                    value = t[r, side, rows]
                    if (at < HALF) == (side != odd):
                        value = value + decode(fwd.at[r, rows])
                    encode(rcv_out.at[r, side, rows], value)
                c_rcv(r, side, 0).start()

        for odd in range(2):
            pl.when(r % 2 == odd)(lambda odd=odd: pass_on(odd))

    def stage2_z(r, q):
        arrived(zf.at[q], zr_sem.at[r])
        for at in range(0, HALF, 16):
            rows = pl.ds(at, 16)
            encode(fwd_out.at[r, rows], t_far[q, mine(at)] + decode(zf.at[q, 0, rows]))
        c_fwd(r, 0, 1).start()
        c_fwd(r, 1, 1).start()
        for rel in range(3):
            for at in range(0, HALF, 16):
                t[r, rel, mine(at)] = t[r, rel, mine(at)] + decode(zf.at[q, 1 + rel, pl.ds(at, 16)])

    def stage3_y(r):
        arrived(rcv.at[r], rcv_sem.at[r])
        for at in range(0, SET, 16):
            rows = pl.ds(at, 16)
            t[r, 2, rows] = t[r, 2, rows] + decode(rcv.at[r, 0, rows]) + decode(rcv.at[r, 1, rows])
        for at in range(0, HALF, 16):
            encode(zr_out.at[r, pl.ds(at, 16)], t[r, 2, others(at)])
        c_zr(r).start()

    def stage3_z(r, q):
        arrived(fwd.at[r, pl.ds(0, HALF)], fwd_sem.at[r])
        for side in range(2):
            for at in range(0, HALF, 16):
                rows = pl.ds(at, 16)
                value = t[r, side, mine(at)]
                if (at >= 48) == (side == 1):
                    value = value + decode(fwd.at[r, rows])
                encode(rcv_out.at[r, side, rows], value)
            c_rcv(r, side, 1).start()

    def exchange(r):
        for d in range(1, 5):
            encode(xr_out.at[r, d - 1], f[r, d])
            if d < 4:
                c_xr(r, d).start()

        @pl.when(zh == 0)
        def _():
            c_xr(r, 4).start()

    def stage4_y(r):
        arrived(zr.at[r], zr_sem.at[r])
        own_rows = pl.ds(pl.multiple_of(HALF * zh, 16), 64)
        theirs = pl.ds(pl.multiple_of(16 * zh, 16), 64)
        f[r, 0:4] = (t[r, 2, own_rows] + decode(zr.at[r, theirs])).reshape(4, 16, QN)
        f[r, 4] = t[r, 2, pl.ds(64, 16)] + decode(zr.at[r, pl.ds(64, 16)])
        exchange(r)

    def stage4_z(r, q):
        arrived(rcv.at[r, :, pl.ds(0, HALF)], rcv_sem.at[r])
        for at in range(0, HALF, 16):
            rows = pl.ds(at, 16)
            t[r, 2, rows] = t[r, 2, mine(at)] + decode(rcv.at[r, 0, rows]) + decode(rcv.at[r, 1, rows])
        f[r, 0:4] = t[r, 2, pl.ds(pl.multiple_of(16 * zh, 16), 64)].reshape(4, 16, QN)
        f[r, 4] = t[r, 2, pl.ds(64, 16)]
        exchange(r)

    def stage5(r):
        @pl.when(zh == 0)
        def _():
            arrived(xr.at[r, 0:3], xr_sem.at[r])

        @pl.when(zh == 1)
        def _():
            arrived(xr.at[r], xr_sem.at[r])

        s, n = r // RN, r % RN
        columns = pl.ds(pl.multiple_of(n * QN, QN), QN)

        def place(block, b, swap):
            for i in range(4):
                for j in range(4):
                    p, q = (j, i) if swap else (i, j)
                    at = (p // 2) * 8 + (q // 2) * 4 + (p % 2) * 2 + q % 2
                    lad_ref[s, pl.ds(i * 32 + b * 4 + j, 1), columns] = block(at)

        def from_f(d):
            return lambda at: f[r, d, pl.ds(at, 1)]

        def from_xr(d):
            value = decode(xr.at[r, d - 1])
            return lambda at: value[at : at + 1]

        def at_of(p, q):
            return (p // 2) * 8 + (q // 2) * 4 + (p % 2) * 2 + q % 2

        for i in range(4):
            for j in range(4):
                lad_ref[s, pl.ds(i * 32 + col * 4 + j, 1), columns] = (
                    f[r, 0, pl.ds(at_of(i, j), 1)] + f[r, 0, pl.ds(at_of(j, i), 1)]
                )
        for d in range(1, 4):
            place(from_f(d), (col + d) % NB, False)
            place(from_xr(d), (col + NB - d) % NB, True)

        @pl.when(zh == 0)
        def _():
            place(from_f(4), (col + 4) % NB, False)

        @pl.when(zh == 1)
        def _():
            place(from_xr(4), (col + 4) % NB, True)

        @pl.when(n == RN - 1)
        def _():
            write(s).start()

    def write(s):
        return pltpu.make_async_copy(lad_ref.at[s], out_hbm.at[s], own_sem.at[s])

    stages = ((stage2_y, stage2_z), (stage3_y, stage3_z), (stage4_y, stage4_z), (stage5, None))

    send_own_z(0)
    send_own_x(0)
    pass_z(0)
    cz(2, own).start()
    send_own_z(1)
    pass_x(0, 0)
    straight(2)
    send_own_x(1)
    cx(0, lefts[1], 0, 1).wait_recv()
    ct(0, lefts[1]).start()
    cx(0, rights[1], 1, 1).wait_recv()
    ct(0, rights[1]).start()
    far_arrived(0, 0)
    cz(0, fars[0], 6).start()
    ct(0, fars[0]).start()
    straight_across(2, 0, own_z)
    straight_pass(2)
    pass_z(1)
    straight_across(0, 6, fars[1])
    load.wait()
    end_twin(0)

    def gather3():
        pass_x(1, 0)

    def gather4():
        straight_far(2)

    def gather6():
        straight_across(2, 1, lefts[1])
        pass_x(1, 1)
        straight_across(2, 2, rights[1])

    def gather7():
        pass_far(1)
        straight_across(2, 3, fars[1])

    def gather8():
        end_twin(1)
        end_twin(2)

    def step(it, carry):
        for when, hook in ((1, gather3), (2, gather4), (4, gather6), (6, gather7), (8, gather8)):
            pl.when(it == when)(hook)

        @pl.when(it < RN)
        def _():
            stage1(it, [(0, e_l)])

        @pl.when((it >= RN + GAP) & (it < ROUNDS + GAP))
        def _():
            one = it < 2 * RN + GAP
            stage1(it - GAP, [(1, jnp.where(one, e_ff, e_fs)), (2, jnp.where(one, e_sf, e_ss))])

        for n in range(4):
            stage, zstage = stages[n]
            lone_r, r, z_r = it - LONE_LAGS[n], it - GAP - LAGS[n], it - GAP - Z_LAGS[n]
            is_lone = (lone_r >= 0) & (lone_r < RN)
            is_pair = (r >= RN) & (r < ROUNDS)
            if zstage is None:
                pl.when(is_lone)(lambda: stage(lone_r))
                pl.when(is_pair)(lambda: stage(r))
            else:
                pl.when(is_lone)(lambda: stage(lone_r))
                pl.when(is_pair & jnp.logical_not(zfirst_of(r)))(lambda: stage(r))
                pl.when(zfirst_of(z_r))(lambda: zstage(z_r, (z_r - RN) // 2))

        return carry

    lax.fori_loop(0, ROUNDS + GAP + LAGS[-1], step, 0)

    end_sends()
    for slot in range(3):
        write(slot).wait()


def ladder_call(tile_pairs, amplitudes, integrals):
    dma = pltpu.SemaphoreType.DMA
    return pl.pallas_call(
        kernel,
        out_shape=jax.ShapeDtypeStruct((3, 128, 1024), jnp.float32),
        in_specs=[
            pl.BlockSpec(memory_space=pltpu.VMEM),
            pl.BlockSpec(memory_space=pl.ANY),
            pl.BlockSpec(memory_space=pl.ANY),
        ],
        out_specs=pl.BlockSpec(memory_space=pl.ANY),
        scratch_shapes=[
            pltpu.VMEM((3, NB, 2, 64, 2048), jnp.bfloat16),
            pltpu.VMEM((5, 2048, 1024), jnp.bfloat16),
            pltpu.VMEM((NB, 2, NB, 8, QN), jnp.float32),
            pltpu.VMEM((ROUNDS, 3, SET, QN), jnp.float32),
            pltpu.VMEM((ZROUNDS, SET, QN), jnp.float32),
            pltpu.VMEM((ROUNDS, SET, WIDE), jnp.bfloat16),
            pltpu.VMEM((ROUNDS, SET, WIDE), jnp.bfloat16),
            pltpu.VMEM((ROUNDS, 2, SET, WIDE), jnp.bfloat16),
            pltpu.VMEM((ROUNDS, 2, SET, WIDE), jnp.bfloat16),
            pltpu.VMEM((ZROUNDS, 4, HALF, WIDE), jnp.bfloat16),
            pltpu.VMEM((ZROUNDS, 4, HALF, WIDE), jnp.bfloat16),
            pltpu.VMEM((ROUNDS, HALF, WIDE), jnp.bfloat16),
            pltpu.VMEM((ROUNDS, HALF, WIDE), jnp.bfloat16),
            pltpu.VMEM((ROUNDS, 5, 16, QN), jnp.float32),
            pltpu.VMEM((ROUNDS, 4, 16, WIDE), jnp.bfloat16),
            pltpu.VMEM((ROUNDS, 4, 16, WIDE), jnp.bfloat16),
            pltpu.VMEM((3, 128, 1024), jnp.float32),
            pltpu.VMEM((3, 64, 2048), jnp.bfloat16),
            dma,
            dma((7,)),
            dma((3, 2, 2)),
            dma((3, 2)),
            dma((3,)),
            dma((ROUNDS,)),
            dma((ROUNDS,)),
            dma((ROUNDS,)),
            dma((ROUNDS,)),
            dma((11,)),
            dma((4,)),
        ],
        compiler_params=pltpu.CompilerParams(
            collective_id=0, has_side_effects=True, vmem_limit_bytes=60 << 20
        ),
        cost_estimate=pl.CostEstimate(flops=21_474_836_480, bytes_accessed=24 << 20, transcendentals=0),
    )(tile_pairs, amplitudes, integrals)


def finish(tp_ref, lad_hbm, drv_hbm, occ_ref, virt_ref, res_hbm, upd_hbm, lad_ref, drv_ref, res_ref, upd_ref, sem):
    row, col = lax.axis_index("row"), lax.axis_index("col")
    lone = read_pairs(tp_ref)[2]
    parts = [(tile, pl.ds(64 * half, 64)) for tile in range(3) for half in range(2)]
    reads = []
    for n, (tile, rows) in enumerate(parts):
        slot = jnp.where(lone == tile, 0, 1 + tile - jnp.where(lone < tile, 1, 0))
        reads.append(pltpu.make_async_copy(lad_hbm.at[slot, rows], lad_ref.at[tile, rows], sem.at[0, n]))
        reads.append(pltpu.make_async_copy(drv_hbm.at[tile, rows], drv_ref.at[tile, rows], sem.at[1, n]))
    for c in reads:
        c.start()
    lanes = occ_ref[...].reshape(1, 32)
    across = lax.broadcasted_iota(jnp.int32, (32, 32), 1)
    eye = lax.broadcasted_iota(jnp.int32, (32, 32), 0) == across
    second = jnp.sum(jnp.where(eye, jnp.broadcast_to(lanes, (32, 32)), 0.0), axis=1, keepdims=True)
    place = lax.broadcasted_iota(jnp.int32, (1, 128), 1)
    sums = []
    for i in range(4):
        here = jnp.sum(jnp.where(across[:1] == col * 4 + i, lanes, 0.0), axis=1, keepdims=True)
        sums.append(jnp.broadcast_to(here + second, (32, 128)))
    for tile in range(3):
        inner, outer = virt_ref[tile, 1:2, :], virt_ref[tile, 0:1, :]
        for c in range(8):
            lead = jnp.sum(jnp.where(place == row * 8 + c, outer, 0.0), axis=1, keepdims=True)
            virtual_pair = lead + inner
            for i in range(4):
                upd_ref[tile, pl.ds(i * 32, 32), pl.ds(c * 128, 128)] = 1.0 / (sums[i] - virtual_pair)
    writes = []
    for n, (tile, rows) in enumerate(parts):
        reads[2 * n].wait()
        reads[2 * n + 1].wait()
        residual = drv_ref[tile, rows].astype(jnp.float32) + lad_ref[tile, rows]
        res_ref[tile, rows] = residual
        upd_ref[tile, rows] = residual * upd_ref[tile, rows]
        writes.append(pltpu.make_async_copy(res_ref.at[tile, rows], res_hbm.at[tile, rows], sem.at[2, n]))
        writes.append(pltpu.make_async_copy(upd_ref.at[tile, rows], upd_hbm.at[tile, rows], sem.at[3, n]))
        writes[-2].start()
        writes[-1].start()
    for c in writes:
        c.wait()


def body(amplitudes, integrals, tile_pairs, driving, occupied_energy, virtual_energy):
    pairs = tile_pairs.T
    ladder = ladder_call(pairs, amplitudes, integrals)
    vmem, anywhere = pl.BlockSpec(memory_space=pltpu.VMEM), pl.BlockSpec(memory_space=pl.ANY)
    out = jax.ShapeDtypeStruct(driving.shape, jnp.float32)
    held = pltpu.VMEM(driving.shape, jnp.float32)
    return pl.pallas_call(
        finish,
        out_shape=[out, out],
        in_specs=[vmem, anywhere, anywhere, vmem, vmem],
        out_specs=[anywhere, anywhere],
        scratch_shapes=[held, pltpu.VMEM(driving.shape, jnp.bfloat16), held, held, pltpu.SemaphoreType.DMA((4, 6))],
        compiler_params=pltpu.CompilerParams(vmem_limit_bytes=60 << 20),
    )(pairs, ladder, driving, occupied_energy, virtual_energy)


def solution(mesh):
    return jax.shard_map(
        body,
        mesh=mesh,
        in_specs=(
            P(None, "row", "col"),
            P(None, "col", "row"),
            P(),
            P(None, "col", "row"),
            P(),
            P(),
        ),
        out_specs=(P(None, "col", "row"), P(None, "col", "row")),
        check_vma=False,
    )
```

profile of v0, /device:TPU:1, one launch (start us, length us, event | category | flops | bytes accessed | tf_op | source)
XLA Modules:
  0.0 106.6 jit_solution(14067030000827818966)
XLA Ops:
  0.6 102.3 %shard_map.77.lad_hbm = f32[3,128,1024]{2,1,0:T(8,128)} custom-call(s32[2,5]{1,0:T(2,128)} %bitcast.1, bf16[3,64,2048]{2,1,0:T(8,128)(2,1)} %amp_hbm.1, bf16[5,2048,1024]{2,1,0:T(8,128)(2,1)} %int_hbm.1), custom_call_target="tpu_custom_call" | custom-call | flops 21474836480 | bytes 25165824 | tf_op jit(solution)/shard_map/pallas_call | solution.py:537
  102.9 3.7 %shard_map.78 = (f32[3,128,1024]{2,1,0:T(8,128)}, f32[3,128,1024]{2,1,0:T(8,128)}) custom-call(s32[2,5]{1,0:T(2,128)} %bitcast.2, f32[3,128,1024]{2,1,0:T(8,128)} %shard_map.77.lad_hbm, bf16[3,128,1024]{2,1,0:T(8,128)(2,1)} %drv_hbm.1, f32[32]{0:T(128)} %occ_ref.1, f32[3,2,128]{2,1,0:T(2,128)} %virt_ref.1), custom_call_target="tpu_custom_call" | custom-call | tf_op jit(solution)/shard_map/pallas_call | solution.py:632
where the time goes:
time: 108 us; the launch traced here: 107 us
  Pallas kernels  106 us (98%)
    pallas_call x1, Pallas kernels, ladder_call(): pl.pallas_call(kernel, out_shape=jax.ShapeDtypeStruct((3, 128, 1024), jnp...  102 us
    pallas_call x1, Pallas kernels, body(): pl.pallas_call(finish, out_shape=[out, out], in_specs=[vmem, anywhere, an...  3.7 us

commit v1 on v0

--- a/solution.py
+++ b/solution.py
@@ -16,7 +16,7 @@
 HALF = 80
 WIDE = QN + QN // 2
 LEVELS = 10
-LONE_LAGS, LAGS, Z_LAGS = (2, 7, 10, 14), (1, 3, 6, 9), (3, 4, 7, 9)
+LONE_LAGS, LAGS, Z_LAGS = (2, 7, 10, 14), (1, 3, 5, 9), (3, 4, 6, 9)
 ZROUNDS = 1
 GAP = 4
 

time: 108 us -> 108 us (level)
  no operation moved by 1% of the time
where the time goes in v1:
time: 108 us; the launch traced here: 107 us
  Pallas kernels  106 us (98%)
    pallas_call x1, Pallas kernels, ladder_call(): pl.pallas_call(kernel, out_shape=jax.ShapeDtypeStruct((3, 128, 1024), jnp...  102 us
    pallas_call x1, Pallas kernels, body(): pl.pallas_call(finish, out_shape=[out, out], in_specs=[vmem, anywhere, an...  3.7 us

profile of v1, /device:TPU:1, one launch (start us, length us, event | category | flops | bytes accessed | tf_op | source)
XLA Modules:
  0.0 106.6 jit_solution(1831765027828886259)
XLA Ops:
  0.6 102.3 %shard_map.77.lad_hbm = f32[3,128,1024]{2,1,0:T(8,128)} custom-call(s32[2,5]{1,0:T(2,128)} %bitcast.1, bf16[3,64,2048]{2,1,0:T(8,128)(2,1)} %amp_hbm.1, bf16[5,2048,1024]{2,1,0:T(8,128)(2,1)} %int_hbm.1), custom_call_target="tpu_custom_call" | custom-call | flops 21474836480 | bytes 25165824 | tf_op jit(solution)/shard_map/pallas_call | solution.py:537
  102.9 3.7 %shard_map.78 = (f32[3,128,1024]{2,1,0:T(8,128)}, f32[3,128,1024]{2,1,0:T(8,128)}) custom-call(s32[2,5]{1,0:T(2,128)} %bitcast.2, f32[3,128,1024]{2,1,0:T(8,128)} %shard_map.77.lad_hbm, bf16[3,128,1024]{2,1,0:T(8,128)(2,1)} %drv_hbm.1, f32[32]{0:T(128)} %occ_ref.1, f32[3,2,128]{2,1,0:T(2,128)} %virt_ref.1), custom_call_target="tpu_custom_call" | custom-call | tf_op jit(solution)/shard_map/pallas_call | solution.py:632
